TPU v7x, 256 devices: a whole 4x4x8 slice. The times are simulated.
256 devices in a mesh: ctx: 32 (over x_lo, z, core), head: 8 (over y, x_hi).
Axes of the slice: x: 4 (x_hi: 2, x_lo: 2; x = x_hi * 2 + x_lo), y: 4, z: 8, core: 2. Of those that a mesh axis runs over, the one named last changes fastest.
Arguments:
- queries: bfloat16 [8192, 2048], P('ctx', 'head'), may hold values from -6 to 6
- keys: bfloat16 [8192, 2048], P('ctx', 'head'), may hold values from -6 to 6
- values: bfloat16 [8192, 2048], P('ctx', 'head'), may hold values from -12 to 12
- frame_mask: int32 [64, 64], replicated, may hold values from 0 to 1, as said below
- out_weight: bfloat16 [2048, 2048], P('head'), may hold values from -0.25 to 0.25
Outputs:
- mixed: bfloat16 [8192, 2048], P(('ctx', 'head'))
Inputs may be any that keep to these rules, and one draw needn't show every extreme that they name: frame_mask[i][j] is 1 for j equal to i and 0 for j greater than i; below the diagonal each entry is 0 or 1.
All inputs are finite; a program needn't handle non-finite values.
Results may differ from a plain program's by a relative error of at most 0.017.
Values may be sent and summed in bfloat16 or wider, within the bound.
A program may use at most 64 MiB of HBM per device.

v0:
```python
import functools
import math

import jax
import jax.numpy as jnp
from jax import lax
from jax.experimental import pallas as pl
from jax.experimental.pallas import tpu as pltpu
from jax.sharding import PartitionSpec as P

HD = 128
FRAME_TOK = 128
NZ = 8
NY = 4
NEG_FILL = -1e30
LOG2E = 1.4426950408889634
MESH = pl.DeviceIdType.MESH


def kernel(
    q_hbm, k_hbm, v_hbm, mask_hbm, w_hbm, out_ref,
    mask, qb, kv, wb, acc, top, ob, ab, pf, ps, pr,
    local_sem, x_send, x_recv, z_send, z_recv, d_send, d_recv, e_send, e_recv,
    w_send, w_recv, c_send, c_recv, o_send, o_recv, p_send, p_recv,
):
    p = lax.axis_index("ctx")
    g = lax.axis_index("head")
    core = lax.rem(p, 2)
    zc = lax.rem(p, 2 * NZ)
    z = lax.div(zc, 2)
    xl = lax.div(p, 2 * NZ)
    y = lax.div(g, 2)
    xh = lax.rem(g, 2)
    rows = q_hbm.shape[0]
    half_cols = w_hbm.shape[1] // 2

    def device(xl_, z_, core_, y_, xh_):
        return ((xl_ * NZ + z_) * 2 + core_, y_ * 2 + xh_)

    def remote(src, dst, send, recv, target):
        return pltpu.make_async_remote_copy(
            src_ref=src, dst_ref=dst, send_sem=send, recv_sem=recv,
            device_id=target, device_id_type=MESH,
        )

    z_up, z_down = lax.rem(z + 1, NZ), lax.rem(z + NZ - 1, NZ)
    y_up, y_down = lax.rem(y + 1, NY), lax.rem(y + NY - 1, NY)
    sibling = device(xl, z, 1 - core, y, xh)
    partner = device(1 - xl, z, core, y, xh)
    up = device(xl, z_up, core, y, xh)
    down = device(xl, z_down, core, y, xh)
    w_up = device(xl, z, core, y_up, xh)
    w_down = device(xl, z, core, y_down, xh)

    def group_member(i):
        h = lax.rem(xl + lax.div(i, NY), 2)
        y_ = lax.rem(y + i, NY)
        return h, y_, device(h, z, core, y_, xh)

    own = pl.ds(pl.multiple_of(xl * HD, HD), HD)
    other = pl.ds(pl.multiple_of((1 - xl) * HD, HD), HD)
    w_cols = pl.ds(pl.multiple_of(core * half_cols, half_cols), half_cols)
    local = [
        pltpu.make_async_copy(k_hbm.at[:, own], kv.at[xl, z, core, 0], local_sem.at[0]),
        pltpu.make_async_copy(v_hbm.at[:, own], kv.at[xl, z, core, 1], local_sem.at[1]),
        pltpu.make_async_copy(q_hbm.at[:, own], qb.at[xl], local_sem.at[2]),
        pltpu.make_async_copy(w_hbm, wb.at[y], local_sem.at[3]),
        pltpu.make_async_copy(mask_hbm, mask, local_sem.at[4]),
    ]
    for copy in local:
        copy.start()

    barrier = pltpu.get_barrier_semaphore()

    def greet(i, carry):
        _, _, target = group_member(i)
        pl.semaphore_signal(barrier, inc=1, device_id=target, device_id_type=MESH)
        return carry

    across = device(xl, z, core, y, 1 - xh)
    for target in (up, down, sibling, across):
        pl.semaphore_signal(barrier, inc=1, device_id=target, device_id_type=MESH)
    lax.fori_loop(1, 2 * NY, greet, 0)
    pl.semaphore_wait(barrier, 11)

    exchange = [
        remote(k_hbm.at[:, other], kv.at[xl, z, core, 0], x_send.at[0], x_recv.at[0], partner),
        remote(v_hbm.at[:, other], kv.at[xl, z, core, 1], x_send.at[1], x_recv.at[1], partner),
        remote(q_hbm.at[:, other], qb.at[xl], x_send.at[2], x_recv.at[2], partner),
    ]
    for copy in exchange[:2]:
        copy.start()

    def ring(direction, h, s):
        if direction == 0:
            unit = kv.at[h, lax.rem(z + NZ - s, NZ), core]
            target = up
        else:
            unit = kv.at[h, lax.rem(z + s, NZ), core]
            target = down
        return remote(
            unit, unit, z_send.at[direction, h, s], z_recv.at[direction, h, s], target
        )

    def ring_end(direction, h):
        piece = kv.at[h, lax.rem(z + (NZ - 3, 3)[direction], NZ), core, direction]
        return remote(
            piece, piece, z_send.at[direction, h, 3], z_recv.at[direction, h, 3],
            (up, down)[direction],
        )

    def share_end(kind, h):
        piece = kv.at[h, source(NZ - 1), core, kind]
        return remote(piece, piece, e_send.at[kind, h], e_recv.at[kind, h], sibling)

    def source(t):
        s = lax.div(t + 1, 2)
        return lax.rem(z + NZ + jnp.where(lax.rem(t, 2) == 1, -s, s), NZ)

    def share(h, t):
        unit = kv.at[h, source(t), core]
        return remote(unit, unit, d_send.at[h, t], d_recv.at[h, t], sibling)

    local[0].wait()
    local[1].wait()
    for direction in (0, 1):
        ring(direction, xl, 0).start()
    share(xl, 0).start()

    w_half = rows // 2
    first, second = pl.ds(0, w_half), pl.ds(w_half, w_half)

    def w_own(i):
        part = (first, second, second, first)[i]
        return remote(
            w_hbm.at[part, w_cols], wb.at[y, part, w_cols], w_send.at[i], w_recv.at[i],
            (w_up, w_down, w_up, w_down)[i],
        )

    def w_forward(i):
        part = (first, second)[i]
        held = wb.at[(y_down, y_up)[i], part, w_cols]
        return remote(held, held, w_send.at[4 + i], w_recv.at[4 + i], (w_up, w_down)[i])

    def w_share(i):
        y_far = lax.rem(y + 2, NY)
        part = (first, second, second, first, first, second)[i]
        held = wb.at[(y_down, y_up, y_down, y_up, y_far, y_far)[i], part, w_cols]
        return remote(held, held, c_send.at[i], c_recv.at[i], sibling)

    for i in range(4):
        w_own(i).start()

    exchange[0].wait_recv()
    exchange[1].wait_recv()
    exchange[2].start()
    for direction in (0, 1):
        ring(direction, 1 - xl, 0).start()
    share(1 - xl, 0).start()

    acc[...] = jnp.zeros_like(acc)
    top[...] = jnp.full(top.shape, NEG_FILL, jnp.float32)

    scale = LOG2E / math.sqrt(HD)
    ones = jnp.ones((2 * rows, HD), jnp.bfloat16)

    def scores(q, half, src):
        k = kv[half, src, :, 0].reshape(2 * rows, HD)
        return lax.dot_general(
            q, k, (((1,), (1,)), ((), ())), preferred_element_type=jnp.float32
        )

    def absorb(h, parts):
        tiles = []
        for half, src in parts:
            s = scores(qb[h], half, src)
            for j in range(2 * rows // FRAME_TOK):
                key_frame = half * 4 * NZ + src * 4 + j
                fill = []
                for f in range(rows // FRAME_TOK):
                    allowed = mask[h * 4 * NZ + zc * 2 + f, key_frame]
                    fill.append(
                        jnp.full(
                            (FRAME_TOK, FRAME_TOK),
                            jnp.where(allowed > 0, 0.0, NEG_FILL),
                            jnp.float32,
                        )
                    )
                tiles.append(
                    s[:, j * FRAME_TOK:(j + 1) * FRAME_TOK] + jnp.concatenate(fill, axis=0)
                )
        best = functools.reduce(jnp.maximum, tiles)
        old_top = top[h]
        new_top = jnp.maximum(old_top, jnp.max(best, axis=1, keepdims=True))
        weights = [jnp.exp2((tile - new_top) * scale).astype(jnp.bfloat16) for tile in tiles]
        fade = jnp.exp2((old_top - new_top) * scale)
        total = acc[h] * jnp.concatenate([fade, fade], axis=1)
        per = 2 * rows // FRAME_TOK
        for i, (half, src) in enumerate(parts):
            v = kv[half, src, :, 1].reshape(2 * rows, HD)
            total += jnp.dot(
                jnp.concatenate(weights[i * per:(i + 1) * per], axis=1),
                jnp.concatenate([v, ones], axis=1),
                preferred_element_type=jnp.float32,
            )
        acc[h] = total
        top[h] = new_top

    def attend(*sources):
        absorb(0, [(0, src) for src in sources])
        absorb(1, [(half, src) for src in sources for half in (0, 1)])

    def step(u, carry):
        s, h = lax.div(u, 2) + 1, lax.rem(xl + u, 2)

        @pl.when(s < 4)
        def _():
            for direction in (0, 1):
                ring(direction, h, s - 1).wait_recv()

                @pl.when(s < 3)
                def _():
                    ring(direction, h, s).start()

                @pl.when(s == 3)
                def _():
                    ring_end(direction, h).start()

                share(h, 2 * s - 1 + direction).start()

        @pl.when(s == 4)
        def _():
            for direction in (0, 1):
                ring_end(direction, h).wait_recv()
                share_end(direction, h).start()

        @pl.when(u == 1)
        def _():
            local[2].wait()
            local[4].wait()
            exchange[2].wait_recv()

        @pl.when(u == 3)
        def _():
            for i in range(2):
                w_own(i).wait_recv()
                w_forward(i).start()
                w_share(i).start()

        @pl.when(u == 5)
        def _():
            for i in range(2, 4):
                w_own(i).wait_recv()
                w_share(i).start()

        @pl.when((u > 0) & (u < NZ))
        def _():
            for h_ in (0, 1):
                share(h_, u - 1).wait_recv()

        @pl.when(u == NZ)
        def _():
            for h_ in (0, 1):
                for kind in (0, 1):
                    share_end(kind, h_).wait_recv()

        @pl.when(u > 0)
        def _():
            attend(source(u - 1))

        return carry

    def pass_on(i):
        h, y_, target = group_member(i)
        return remote(
            ob.at[h, y_], ab.at[y, xl], o_send.at[i], o_recv.at[i], target
        )

    def end_pass(i, carry):
        pass_on(i).wait_recv()
        return carry

    lax.fori_loop(0, NZ + 1, step, 0)
    def conclude(i, carry):
        h = lax.rem(xl + 1 + i, 2)
        done = (acc[h, :, :HD] / acc[h, :, HD:]).astype(jnp.bfloat16)
        ob[h] = done.reshape(NY, rows // NY, HD)

        def start_pass(j, carry):
            pass_on((1 - i) * NY + j).start()
            return carry

        lax.fori_loop(i, NY, start_pass, 0)
        return carry

    lax.fori_loop(0, 2, conclude, 0)
    ab[y, xl] = ob[xl, y]

    for i in range(2):
        w_forward(i).wait_recv()
        w_share(4 + i).start()

    for copy in exchange:
        copy.wait_send()
    for i in range(4):
        w_own(i).wait_send()
    for i in range(2):
        w_forward(i).wait_send()
    for i in range(6):
        w_share(i).wait_send()
        w_share(i).wait_recv()
    local[3].wait()

    def end_ring(s, carry):
        for direction in (0, 1):
            for h in (0, 1):
                ring(direction, h, s).wait_send()
        return carry

    def end_share(t, carry):
        share(0, t).wait_send()
        share(1, t).wait_send()
        return carry

    lax.fori_loop(0, 3, end_ring, 0)
    lax.fori_loop(0, NZ - 1, end_share, 0)
    for direction in (0, 1):
        for h in (0, 1):
            ring_end(direction, h).wait_send()
            share_end(direction, h).wait_send()
    lax.fori_loop(1, 2 * NY, end_pass, 0)

    attended = jnp.concatenate([ab[i, j] for i in range(NY) for j in range(2)], axis=1)
    out_rows, width = out_ref.shape
    block = width // 4

    def hand_over(i):
        cols = pl.ds(pl.multiple_of(i * block, block), block)
        return remote(
            ps.at[1 - xh, :, cols], pr.at[:, cols], p_send.at[i], p_recv.at[i], across
        )

    def project(i, carry):
        cols = pl.ds(pl.multiple_of(i * block, block), block)
        part = jnp.dot(
            attended, wb[:, :, cols].reshape(NY * rows, block),
            preferred_element_type=jnp.float32,
        ).reshape(2, out_rows, block)
        pf[:, :, cols] = part
        ps[:, :, cols] = part.astype(jnp.bfloat16)
        hand_over(i).start()
        return carry

    lax.fori_loop(0, 4, project, 0)

    def end_send(i, carry):
        pass_on(i).wait_send()
        return carry

    lax.fori_loop(1, 2 * NY, end_send, 0)
    def finish(i, carry):
        cols = pl.ds(pl.multiple_of(i * block, block), block)
        hand_over(i).wait_recv()
        out_ref[:, cols] = (
            pf[xh, :, cols] + pr[:, cols].astype(jnp.float32)
        ).astype(out_ref.dtype)
        return carry

    lax.fori_loop(0, 4, finish, 0)
    for i in range(4):
        hand_over(i).wait_send()


def on_device(queries, keys, values, frame_mask, out_weight):
    rows = queries.shape[0]
    width = out_weight.shape[1]
    out_rows = rows // (2 * NY)
    hbm_spec = pl.BlockSpec(memory_space=pltpu.HBM)
    dma = pltpu.SemaphoreType.DMA
    bf16, f32 = jnp.bfloat16, jnp.float32
    return pl.pallas_call(
        kernel,
        out_shape=jax.ShapeDtypeStruct((out_rows, width), bf16),
        in_specs=[hbm_spec] * 5,
        out_specs=pl.BlockSpec(memory_space=pltpu.VMEM),
        scratch_shapes=[
            pltpu.SMEM(frame_mask.shape, frame_mask.dtype),
            pltpu.VMEM((2, rows, HD), bf16),
            pltpu.VMEM((2, NZ, 2, 2, rows, HD), bf16),
            pltpu.VMEM((NY, rows, width), bf16),
            pltpu.VMEM((2, rows, 2 * HD), f32),
            pltpu.VMEM((2, rows, HD), f32),
            pltpu.VMEM((2, NY, rows // NY, HD), bf16),
            pltpu.VMEM((NY, 2, rows // NY, HD), bf16),
            pltpu.VMEM((2, out_rows, width), f32),
            pltpu.VMEM((2, out_rows, width), bf16),
            pltpu.VMEM((out_rows, width), bf16),
            dma((5,)),
            dma((3,)), dma((3,)),
            dma((2, 2, 4)), dma((2, 2, 4)),
            dma((2, NZ)), dma((2, NZ)),
            dma((2, 2)), dma((2, 2)),
            dma((6,)), dma((6,)),
            dma((6,)), dma((6,)),
            dma((2 * NY,)), dma((2 * NY,)),
            dma((4,)), dma((4,)),
        ],
        compiler_params=pltpu.CompilerParams(
            collective_id=0, has_side_effects=True, vmem_limit_bytes=55040 * 1024
        ),
        cost_estimate=pl.CostEstimate(
            flops=3 * 10**9, bytes_accessed=10 * 2**20, transcendentals=4 * 2**20
        ),
    )(queries, keys, values, frame_mask, out_weight)


def solution(mesh):
    return jax.shard_map(
        on_device,
        mesh=mesh,
        in_specs=(P("ctx", "head"), P("ctx", "head"), P("ctx", "head"), P(), P("head", None)),
        out_specs=P(("ctx", "head"), None),
        check_vma=False,
    )
```

profile of v0, /device:TPU:1, one launch (start us, length us, event | category | flops | bytes accessed | tf_op | source)
XLA Modules:
  0.0 46.5 jit_solution(2197664131559653000)
XLA Ops:
  0.0 0.0 copy-start
  0.0 0.8 %copy-done = s32[64,64]{1,0:T(8,128)S(1)} copy-done((s32[64,64]{1,0:T(8,128)S(1)}, s32[64,64]{1,0:T(8,128)}, u32[]{:S(2)}) %copy-start) | copy-done | bytes 16408
  0.8 45.1 %shard_map.55 = bf16[32,2048]{1,0:T(8,128)(2,1)S(1)} custom-call(bf16[256,256]{1,0:T(8,128)(2,1)} %q_hbm.1, bf16[256,256]{1,0:T(8,128)(2,1)} %k_hbm.1, bf16[256,256]{1,0:T(8,128)(2,1)} %v_hbm.1, s32[64,64]{1,0:T(8,128)S(1)} %copy-done, bf16[256,2048]{1,0:T(8,128)(2,1)} %w_hbm.1), custom_call_target="tpu_custom_call" | custom-call | flops 3000000000 | bytes 10485760 | tf_op jit(solution)/shard_map/pallas_call | solution.py:381
  45.9 0.7 %copy.7 = bf16[32,2048]{1,0:T(8,128)(2,1)} copy(bf16[32,2048]{1,0:T(8,128)(2,1)S(1)} %shard_map.55) | data formatting | bytes 262144
Async XLA Ops:
  0.0 0.8 %copy-start = (s32[64,64]{1,0:T(8,128)S(1)}, s32[64,64]{1,0:T(8,128)}, u32[]{:S(2)}) copy-start(s32[64,64]{1,0:T(8,128)} %mask_hbm.1) | copy-start | bytes 49156
where the time goes:
time: 46.7 us; the launch traced here: 46.5 us
  Pallas kernels  45.1 us (97%)
  local copies, waits for them, and re-layouts  1.42 us (3%)
    pallas_call x1, Pallas kernels, on_device(): pl.pallas_call(kernel, out_shape=jax.ShapeDtypeStruct((out_rows, width),...  45.1 us
    unnamed x3, local copies, waits for them, and re-layouts  1.42 us

commit v1 on v0

--- a/solution.py
+++ b/solution.py
@@ -77,7 +77,7 @@
         pl.semaphore_signal(barrier, inc=1, device_id=target, device_id_type=MESH)
         return carry
 
-    across = device(xl, z, core, y, 1 - xh)
+    across = device(1 - xl, z, core, y, 1 - xh)
     for target in (up, down, sibling, across):
         pl.semaphore_signal(barrier, inc=1, device_id=target, device_id_type=MESH)
     lax.fori_loop(1, 2 * NY, greet, 0)
@@ -281,19 +281,21 @@
         return carry
 
     lax.fori_loop(0, NZ + 1, step, 0)
-    def conclude(i, carry):
-        h = lax.rem(xl + 1 + i, 2)
-        done = (acc[h, :, :HD] / acc[h, :, HD:]).astype(jnp.bfloat16)
-        ob[h] = done.reshape(NY, rows // NY, HD)
-
-        def start_pass(j, carry):
-            pass_on((1 - i) * NY + j).start()
-            return carry
-
-        lax.fori_loop(i, NY, start_pass, 0)
+    def conclude(h, carry):
+        done = (acc[h, :, :HD] / acc[h, :, HD:]).astype(jnp.bfloat16).reshape(
+            NY, 2, rows // (2 * NY), HD
+        )
+        for x_ in (0, 1):
+            away = jnp.where(xh == x_, 0, 1)
+            ob[jnp.where(xh == x_, h, 1 - h), :, away] = done[:, x_]
+        return carry
+
+    def start_pass(i, carry):
+        pass_on(2 * NY - 1 - i).start()
         return carry
 
     lax.fori_loop(0, 2, conclude, 0)
+    lax.fori_loop(0, 2 * NY - 1, start_pass, 0)
     ab[y, xl] = ob[xl, y]
 
     for i in range(2):
@@ -330,14 +332,14 @@
             share_end(direction, h).wait_send()
     lax.fori_loop(1, 2 * NY, end_pass, 0)
 
-    attended = jnp.concatenate([ab[i, j] for i in range(NY) for j in range(2)], axis=1)
+    attended = jnp.concatenate([ab[i, j].reshape(rows // NY, HD) for i in range(NY) for j in range(2)], axis=1)
     out_rows, width = out_ref.shape
     block = width // 4
 
     def hand_over(i):
         cols = pl.ds(pl.multiple_of(i * block, block), block)
         return remote(
-            ps.at[1 - xh, :, cols], pr.at[:, cols], p_send.at[i], p_recv.at[i], across
+            ps.at[:, cols], pr.at[:, cols], p_send.at[i], p_recv.at[i], across
         )
 
     def project(i, carry):
@@ -346,9 +348,9 @@
             attended, wb[:, :, cols].reshape(NY * rows, block),
             preferred_element_type=jnp.float32,
         ).reshape(2, out_rows, block)
-        pf[:, :, cols] = part
-        ps[:, :, cols] = part.astype(jnp.bfloat16)
+        ps[:, cols] = part[1].astype(jnp.bfloat16)
         hand_over(i).start()
+        pf[:, cols] = part[0]
         return carry
 
     lax.fori_loop(0, 4, project, 0)
@@ -362,7 +364,7 @@
         cols = pl.ds(pl.multiple_of(i * block, block), block)
         hand_over(i).wait_recv()
         out_ref[:, cols] = (
-            pf[xh, :, cols] + pr[:, cols].astype(jnp.float32)
+            pf[:, cols] + pr[:, cols].astype(jnp.float32)
         ).astype(out_ref.dtype)
         return carry
 
@@ -390,10 +392,10 @@
             pltpu.VMEM((NY, rows, width), bf16),
             pltpu.VMEM((2, rows, 2 * HD), f32),
             pltpu.VMEM((2, rows, HD), f32),
-            pltpu.VMEM((2, NY, rows // NY, HD), bf16),
-            pltpu.VMEM((NY, 2, rows // NY, HD), bf16),
-            pltpu.VMEM((2, out_rows, width), f32),
-            pltpu.VMEM((2, out_rows, width), bf16),
+            pltpu.VMEM((2, NY, 2, out_rows, HD), bf16),
+            pltpu.VMEM((NY, 2, 2, out_rows, HD), bf16),
+            pltpu.VMEM((out_rows, width), f32),
+            pltpu.VMEM((out_rows, width), bf16),
             pltpu.VMEM((out_rows, width), bf16),
             dma((5,)),
             dma((3,)), dma((3,)),

time: 46.7 us -> 46.4 us (level)
  no operation moved by 1% of the time
where the time goes in v1:
time: 46.4 us; the launch traced here: 46.3 us
  Pallas kernels  44.8 us (97%)
  local copies, waits for them, and re-layouts  1.42 us (3%)
    pallas_call x1, Pallas kernels, on_device(): pl.pallas_call(kernel, out_shape=jax.ShapeDtypeStruct((out_rows, width),...  44.8 us
    unnamed x3, local copies, waits for them, and re-layouts  1.42 us

profile of v1, /device:TPU:1, one launch (start us, length us, event | category | flops | bytes accessed | tf_op | source)
XLA Modules:
  0.0 46.3 jit_solution(6351942163976328954)
XLA Ops:
  0.0 0.0 copy-start
  0.0 0.8 %copy-done = s32[64,64]{1,0:T(8,128)S(1)} copy-done((s32[64,64]{1,0:T(8,128)S(1)}, s32[64,64]{1,0:T(8,128)}, u32[]{:S(2)}) %copy-start) | copy-done | bytes 16408
  0.8 44.8 %shard_map.55 = bf16[32,2048]{1,0:T(8,128)(2,1)S(1)} custom-call(bf16[256,256]{1,0:T(8,128)(2,1)} %q_hbm.1, bf16[256,256]{1,0:T(8,128)(2,1)} %k_hbm.1, bf16[256,256]{1,0:T(8,128)(2,1)} %v_hbm.1, s32[64,64]{1,0:T(8,128)S(1)} %copy-done, bf16[256,2048]{1,0:T(8,128)(2,1)} %w_hbm.1), custom_call_target="tpu_custom_call" | custom-call | flops 3000000000 | bytes 10485760 | tf_op jit(solution)/shard_map/pallas_call | solution.py:383
  45.6 0.7 %copy.7 = bf16[32,2048]{1,0:T(8,128)(2,1)} copy(bf16[32,2048]{1,0:T(8,128)(2,1)S(1)} %shard_map.55) | data formatting | bytes 262144
Async XLA Ops:
  0.0 0.8 %copy-start = (s32[64,64]{1,0:T(8,128)S(1)}, s32[64,64]{1,0:T(8,128)}, u32[]{:S(2)}) copy-start(s32[64,64]{1,0:T(8,128)} %mask_hbm.1) | copy-start | bytes 49156
